TPU v7x, 32 devices: a whole 2x2x4 slice. The times are simulated.
32 devices in a mesh: dp: 16 (over z, y, core), tensor: 2 (over x).
Axes of the slice: x: 2, y: 2, z: 4, core: 2. Of those that a mesh axis runs over, the one named last changes fastest.
Arguments:
- cotangent: bfloat16 [16384, 3072], P(('dp', 'tensor')), may hold values from -6 to 6
- context: bfloat16 [16384, 3072], P('dp', 'tensor'), may hold values from -6 to 6
- master: float32 [3072, 3072], P('dp', 'tensor'), may hold values from -0.109375 to 0.109375
- first_moment: float32 [3072, 3072], P('dp', 'tensor'), may hold values from -0.046875 to 0.046875
- second_moment: float32 [3072, 3072], P('dp', 'tensor'), as said below
Outputs:
- d_context: bfloat16 [16384, 3072], P('dp', 'tensor')
- new_master: float32 [3072, 3072], P('dp', 'tensor')
- new_first: float32 [3072, 3072], P('dp', 'tensor')
- new_second: float32 [3072, 3072], P('dp', 'tensor')
- new_weights: bfloat16 [3072, 3072], P(None, 'tensor')
Inputs may be any that keep to these rules, and one draw needn't show every extreme that they name: second_moment is positive.
All inputs are finite; a program needn't handle non-finite values.
Results may differ from a plain program's by a relative error of at most 0.0049.
Values may be sent and summed in bfloat16 or wider, within the bound.
A program may use at most 128 MiB of HBM per device.

v0:
```python
import jax
import jax.numpy as jnp
from jax import lax
from jax.sharding import PartitionSpec as P

STEP = 10


def input_gradient(rows_all, weights):
    gathered = lax.all_gather(weights, "dp", axis=0, tiled=True)
    total = jnp.dot(rows_all, gathered, preferred_element_type=jnp.float32)
    return total.astype(jnp.bfloat16)


def owned_gradient(rows_all, context):
    return lax.psum_scatter(
        lax.dot_general(
            rows_all, context, (((0,), (0,)), ((), ())), preferred_element_type=jnp.float32
        ),
        "dp",
        scatter_dimension=0,
        tiled=True,
    )


def body(cotangent, context, master, first_moment, second_moment):
    owners = lax.axis_size("dp")
    token_count = context.shape[0] * owners
    rows_all = lax.all_gather(cotangent, "tensor", axis=0, tiled=True)
    weights = master.astype(jnp.bfloat16)
    d_context = input_gradient(rows_all, weights)
    summed = owned_gradient(rows_all, context)
    grad = summed / jnp.float32(token_count)
    new_first = 0.9 * first_moment + 0.1 * grad
    new_second = 0.95 * second_moment + 0.05 * grad * grad
    first_scale = 1.0 - 0.9**STEP
    second_scale = 1.0 - 0.95**STEP
    update = new_first / first_scale / (jnp.sqrt(new_second / second_scale) + 1e-08)
    new_master = master - 0.001 * update
    new_weights = lax.all_gather(new_master.astype(jnp.bfloat16), "dp", axis=0, tiled=True)
    return (d_context, new_master, new_first, new_second, new_weights)


def solution(mesh):
    in_specs = (
        P(("dp", "tensor"), None),
        P("dp", "tensor"),
        P("dp", "tensor"),
        P("dp", "tensor"),
        P("dp", "tensor"),
    )
    out_specs = (
        P("dp", "tensor"),
        P("dp", "tensor"),
        P("dp", "tensor"),
        P("dp", "tensor"),
        P(None, "tensor"),
    )
    return jax.shard_map(body, mesh=mesh, in_specs=in_specs, out_specs=out_specs, check_vma=False)
```

profile of v0, /device:TPU:0, one launch (start us, length us, event | category | flops | bytes accessed | tf_op | source)
XLA Modules:
  0.0 485.6 jit_solution(13269712328121700211)
XLA Ops:
  7.2 0.0 copy-start
  7.2 0.0 all-gather.4.cloned.1.call-start
  7.2 0.7 all-gather.4.cloned.1.call-update
  7.9 0.0 reduce-scatter.2.cloned.1.call-start
  8.0 84.7 %all-gather.4.cloned.1.call-done = bf16[1024,3072]{1,0:T(8,128)(2,1)} async-done(((bf16[512,3072]{1,0:T(8,128)(2,1)}), bf16[1024,3072]{1,0:T(8,128)(2,1)}) %all-gather.4.cloned.1.call-update) | async-done | bytes 6291472 | tf_op jit(solution)/shard_map/all_gather | solution.py:29
  92.7 0.0 copy-done
  92.7 15.8 %fusion.1 = f32[3072,1536]{1,0:T(8,128)} fusion(bf16[1024,3072]{1,0:T(8,128)(2,1)} %all-gather.4.cloned.1.call-done, bf16[1024,1536]{1,0:T(8,128)(2,1)S(1)} %copy-done), kind=kOutput, calls=%fused_computation.5 | convolution fusion | flops 9663676416 | bytes 28311552 | tf_op jit(solution)/shard_map/dot_general | solution.py:17
  108.4 0.0 copy-start.2
  108.4 0.0 copy-start.3
  108.4 0.0 reduce-scatter.2.cloned.1.call-update
  108.5 0.0 all-gather.6.cloned.1.call-start
  108.5 194.9 %reduce-scatter.2.cloned.1.call-done = f32[192,1536]{1,0:T(8,128)} async-done(((f32[3072,1536]{1,0:T(8,128)}), f32[192,1536]{1,0:T(8,128)}) %reduce-scatter.2.cloned.1.call-update) | async-done | bytes 1179664 | tf_op jit(solution)/shard_map/reduce_scatter | solution.py:16
  303.4 0.0 copy-done.2
  303.4 0.0 copy-done.3
  303.4 4.4 fusion
  307.8 0.0 all-gather.6.cloned.1.call-update
  307.8 0.0 all-gather.8.cloned.1.call-start
  307.9 0.5 all-gather.8.cloned.1.call-update
  308.4 80.1 %all-gather.6.cloned.1.call-done = bf16[3072,1536]{1,0:T(8,128)(2,1)} async-done(((bf16[192,1536]{1,0:T(8,128)(2,1)}), bf16[3072,1536]{1,0:T(8,128)(2,1)}) %all-gather.6.cloned.1.call-update) | async-done | bytes 9437200 | tf_op jit(solution)/shard_map/all_gather | solution.py:10
  388.5 15.4 %convolution_convert_fusion = bf16[1024,1536]{1,0:T(8,128)(2,1)} fusion(bf16[1024,3072]{1,0:T(8,128)(2,1)} %all-gather.4.cloned.1.call-done, bf16[3072,1536]{1,0:T(8,128)(2,1)} %all-gather.6.cloned.1.call-done), kind=kOutput, calls=%fused_computation | convolution fusion | flops 9665249280 | bytes 18874368 | tf_op jit(solution)/shard_map/dot_general | solution.py:11
  404.0 66.9 %all-gather.8.cloned.1.call-done = bf16[3072,1536]{1,0:T(8,128)(2,1)} async-done(((bf16[192,1536]{1,0:T(8,128)(2,1)}), bf16[3072,1536]{1,0:T(8,128)(2,1)}) %all-gather.8.cloned.1.call-update) | async-done | bytes 9437200 | tf_op jit(solution)/shard_map/all_gather | solution.py:40
  470.9 0.0 copy-start.1
  470.9 8.2 %copy.11 = bf16[3072,1536]{1,0:T(8,128)(2,1)} copy(bf16[3072,1536]{1,0:T(8,128)(2,1)} %all-gather.8.cloned.1.call-done) | data formatting | bytes 18874368
  479.0 0.0 copy-done.1
Async XLA Ops:
  7.2 85.5 %copy-start = (bf16[1024,1536]{1,0:T(8,128)(2,1)S(1)}, bf16[1024,1536]{1,0:T(8,128)(2,1)}, u32[]{:S(2)}) copy-start(bf16[1024,1536]{1,0:T(8,128)(2,1)} %param.6) | copy-start | bytes 9437188
  7.2 85.5 %all-gather.4.cloned.1.call-start = ((), (), s32[]{:S(2)}) async-start(), calls=%async_computation.1 | async-start | bytes 9437184 | tf_op jit(solution)/shard_map/all_gather | solution.py:29
  7.9 295.5 %reduce-scatter.2.cloned.1.call-start = ((), (), s32[]{:S(2)}) async-start(), calls=%async_computation.3 | async-start | bytes 20054016 | tf_op jit(solution)/shard_map/reduce_scatter | solution.py:16
  108.4 195.0 %copy-start.2 = (f32[192,1536]{1,0:T(8,128)S(1)}, f32[192,1536]{1,0:T(8,128)}, u32[]{:S(2)}) copy-start(f32[192,1536]{1,0:T(8,128)} %param.7) | copy-start | bytes 3538948
  108.4 195.0 %copy-start.3 = (f32[192,1536]{1,0:T(8,128)S(1)}, f32[192,1536]{1,0:T(8,128)}, u32[]{:S(2)}) copy-start(f32[192,1536]{1,0:T(8,128)} %param.8) | copy-start | bytes 3538948
  108.5 280.1 %all-gather.6.cloned.1.call-start = ((), (), s32[]{:S(2)}) async-start(), calls=%async_computation.2 | async-start | bytes 10027008 | tf_op jit(solution)/shard_map/all_gather | solution.py:10
  307.8 163.0 %all-gather.8.cloned.1.call-start = ((), (), s32[]{:S(2)}) async-start(), calls=%async_computation.4 | async-start | bytes 10027008 | tf_op jit(solution)/shard_map/all_gather | solution.py:40
  470.9 8.2 %copy-start.1 = (bf16[1024,1536]{1,0:T(8,128)(2,1)S(1)}, bf16[1024,1536]{1,0:T(8,128)(2,1)}, u32[]{:S(2)}) copy-start(bf16[1024,1536]{1,0:T(8,128)(2,1)} %param.6) | copy-start | bytes 9437188
Sparse Core Ops, SparseCore 0:
  9.6 83.0 all-gather.3
  108.6 194.7 reduce-scatter.1
  308.0 80.5 all-gather.5
  391.2 79.5 all-gather.7
where the time goes:
time: 486 us
  waiting for transfers between devices  428 us (88%)
  matrix products  31.2 us (6%)
  between operations  13.8 us (3%)
  local copies, waits for them, and re-layouts  8.21 us (2%)
    reduce_scatter x1, waiting for transfers between devices, owned_gradient(): lax.psum_scatter(lax.dot_general(rows_all, context, (((0,), (0,)), ((), (...  195 us
    all_gather x1, waiting for transfers between devices, body(): rows_all = lax.all_gather(cotangent, 'tensor', axis=0, tiled=True)  84.7 us
    all_gather x1, waiting for transfers between devices, input_gradient(): gathered = lax.all_gather(weights, 'dp', axis=0, tiled=True)  80.1 us
    all_gather x1, waiting for transfers between devices, body(): lax.all_gather(new_master.astype(jnp.bfloat16), 'dp', axis=0, tiled=True)  66.9 us
    dot_general x1, matrix products, owned_gradient(): lax.dot_general(rows_all, context, (((0,), (0,)), ((), ())), preferred_el...  15.8 us
    dot_general x1, matrix products, input_gradient(): total = jnp.dot(rows_all, gathered, preferred_element_type=jnp.float32)  15.4 us
  transfers between devices with their start and end apart: 4, of which 4 were waited for; matrix products, arithmetic and copies ran while one was open for 3% of the time, Pallas kernels for 0%

commit v1 on v0

v1 whole, which is shorter than its diff:
```python
import functools

import jax
import jax.numpy as jnp
from jax import lax
from jax.experimental import pallas as pl
from jax.experimental.pallas import tpu as pltpu
from jax.sharding import PartitionSpec as P

STEP = 10
F32 = jnp.float32
BF16 = jnp.bfloat16


def tile_of(extent, most):
    best = extent
    for size in range(128, most + 1, 128):
        if extent % size == 0:
            best = size
    return best if best <= most else extent


def kernel(
    A, B, T, tokens,
    cot, ctx_in, mas, mom, var,
    dctx, nmas, nmom, nvar, nw,
    ctx, cotg, wfull, own, s1, r1, qown, s2, r2, s3, r3, nown,
    loc_sem, cs_sem, cr_sem, ws_sem, wr_sem, ns_sem, nr_sem,
    s1_sem, r1_sem, s2_sem, r2_sem, s3_sem, r3_sem,
):
    G = A * B
    R, N = mas.shape
    tk = ctx.shape[1]
    nt = tile_of(N, 512)
    me = lax.axis_index("dp")
    t = lax.axis_index("tensor")
    chip = me // 2
    c = me % 2
    a = chip // B
    b = chip % B

    def flat(a_, b_, c_):
        return (a_ * B + b_) * 2 + c_

    a_of = [lax.rem(a + i, A) for i in range(A)]
    b_of = [lax.rem(b + i, B) for i in range(B)]
    t_of = [lax.rem(t + i, T) for i in range(T)]
    sib = flat(a, b, 1 - c)
    sends = []

    def send(src, dst, ssem, rsem, where):
        copy = pltpu.make_async_remote_copy(
            src_ref=src, dst_ref=dst, send_sem=ssem, recv_sem=rsem,
            device_id=where, device_id_type=pl.DeviceIdType.MESH,
        )
        copy.start()
        sends.append(copy)

    def arrived(dst, ssem, rsem):
        pltpu.make_async_remote_copy(
            src_ref=dst, dst_ref=dst, send_sem=ssem, recv_sem=rsem,
            device_id={"dp": sib}, device_id_type=pl.DeviceIdType.MESH,
        ).wait_recv()

    barrier = pltpu.get_barrier_semaphore()
    peers = [{"dp": flat(a_of[i], b, c)} for i in range(1, A)]
    peers += [{"dp": flat(a, b_of[i], c)} for i in range(1, B)]
    peers += [{"dp": sib}]
    peers += [{"tensor": t_of[i]} for i in range(1, T)]
    for where in peers:
        pl.semaphore_signal(barrier, inc=1, device_id=where, device_id_type=pl.DeviceIdType.MESH)
    pl.semaphore_wait(barrier, len(peers))

    order = [(ai, bi) for ai in [*range(1, A), 0] for bi in [*range(1, B), 0]]

    def group(k):
        ai, bi = order[k]
        return a_of[ai] * B + b_of[bi]

    def exchange(k):
        g = group(k)
        for i in range(1, T):
            send(cot.at[g], cotg.at[t, g], cs_sem.at[k, i - 1], cr_sem.at[k, i - 1], {"tensor": t_of[i]})

    ahead = 3
    for k in range(min(ahead, G)):
        exchange(k)
    ctx_copy = pltpu.make_async_copy(ctx_in, ctx, loc_sem.at[0])
    ctx_copy.start()
    cot_copy = pltpu.make_async_copy(cot, cotg.at[t], loc_sem.at[1])
    cot_copy.start()

    class Gather:
        def __init__(self, src, buf, ssem, rsem):
            self.src, self.buf, self.ssem, self.rsem, self.n = src, buf, ssem, rsem, 0

        def put(self, src, d, where):
            send(src, self.buf.at[d], self.ssem.at[self.n], self.rsem.at[d], {"dp": where})
            self.n += 1

        def first(self):
            for i in range(1, A):
                self.put(self.src, me, flat(a_of[i], b, c))
            for i in range(1, B):
                self.put(self.src, me, flat(a, b_of[i], c))
            self.put(self.src, me, sib)

        def wait(self, d):
            arrived(self.buf.at[d], self.ssem.at[0], self.rsem.at[d])

        def along_a(self, i):
            d = flat(a_of[A - i], b, c)
            self.wait(d)
            for j in range(1, B):
                self.put(self.buf.at[d], d, flat(a, b_of[j], c))
            self.put(self.buf.at[d], d, sib)

        def along_b(self, i):
            for j in range(1, B):
                d = flat(a_of[(A - i) % A], b_of[j], c)
                self.wait(d)
                self.put(self.buf.at[d], d, sib)

        def last(self):
            for i in range(A):
                for j in range(B):
                    self.wait(flat(a_of[i], b_of[j], 1 - c))

    wfull[me] = mas[...].astype(BF16)
    weights = Gather(wfull.at[me], wfull, ws_sem, wr_sem)
    weights.first()
    ctx_copy.wait()
    cot_copy.wait()

    def partial(g, core, store):
        def tile(n, carry):
            cols = pl.ds(pl.multiple_of(n * nt, nt), nt)
            total = jnp.dot(cotg[0, g, core], ctx[0, :, cols], preferred_element_type=F32)
            for i in range(1, T):
                total = total + jnp.dot(cotg[i, g, core], ctx[i, :, cols], preferred_element_type=F32)
            store(cols, total)
            return carry

        lax.fori_loop(0, N // nt, tile, 0)

    def stage2(k):
        ai, bi = order[k]
        arrived(r1.at[k], s1_sem.at[k], r1_sem.at[k])
        q = own[k % 2] + r1[k].astype(F32)
        if bi:
            j = ai * (B - 1) + bi - 1
            s2[j] = q.astype(BF16)
            send(s2.at[j], r2.at[j], s2_sem.at[j], r2_sem.at[j], {"dp": flat(a, b_of[bi], c)})
        else:
            qown[ai % 2] = q

    def stage3(ai):
        q = qown[ai % 2]
        for bi in range(1, B):
            j = ai * (B - 1) + bi - 1
            arrived(r2.at[j], s2_sem.at[j], r2_sem.at[j])
            q = q + r2[j].astype(F32)
        if ai:
            s3[ai - 1] = q.astype(BF16)
            send(s3.at[ai - 1], r3.at[ai - 1], s3_sem.at[ai - 1], r3_sem.at[ai - 1], {"dp": flat(a_of[ai], b, c)})
        return q

    forwarded = 0
    for k in range(G):
        g = group(k)
        for i in range(1, T):
            arrived(cotg.at[t_of[T - i], g], cs_sem.at[k, i - 1], cr_sem.at[k, i - 1])
        if k + ahead < G:
            exchange(k + ahead)

        def to_sibling(cols, total):
            s1[k, :, cols] = total.astype(BF16)

        def to_own(cols, total):
            own[k % 2, :, cols] = total

        partial(g, 1 - c, to_sibling)
        send(s1.at[k], r1.at[k], s1_sem.at[k], r1_sem.at[k], {"dp": sib})
        partial(g, c, to_own)
        if k:
            stage2(k - 1)
        if k % B == B - 1 and k // B >= 1:
            stage3(order[k - B][0])
        if (k + 1) * (A - 1) // G > forwarded:
            forwarded += 1
            weights.along_a(forwarded)
    stage2(G - 1)
    q = stage3(0)
    for i in range(1, A):
        arrived(r3.at[i - 1], s3_sem.at[i - 1], r3_sem.at[i - 1])
        q = q + r3[i - 1].astype(F32)

    grad = q / jnp.float32(tokens)
    new_first = 0.9 * mom[...] + 0.1 * grad
    new_second = 0.95 * var[...] + 0.05 * grad * grad
    update = new_first / (1.0 - 0.9**STEP) / (jnp.sqrt(new_second / (1.0 - 0.95**STEP)) + 1e-08)
    new_master = mas[...] - 0.001 * update
    nown[...] = new_master.astype(BF16)
    fresh = Gather(nown, nw, ns_sem, nr_sem)
    fresh.first()
    nmom[...] = new_first
    nvar[...] = new_second
    nmas[...] = new_master
    own_copy = pltpu.make_async_copy(nown, nw.at[me], loc_sem.at[0])
    own_copy.start()

    for i in range(A):
        weights.along_b(i)
    weights.last()

    mt = tile_of(tk, 256)

    def columns(n):
        cols = pl.ds(pl.multiple_of(n * nt, nt), nt)

        def tile(i, carry):
            rows = pl.ds(pl.multiple_of((i % (tk // mt)) * mt, mt), mt)
            left = cotg[i // (tk // mt), :, :, :, rows].reshape(G * 2 * R, mt)
            right = wfull[:, :, cols].reshape(G * 2 * R, nt)
            total = lax.dot_general(left, right, (((0,), (0,)), ((), ())), preferred_element_type=F32)
            dctx[pl.ds(pl.multiple_of(i * mt, mt), mt), cols] = total.astype(BF16)
            return carry

        lax.fori_loop(0, T * (tk // mt), tile, 0)

    steps = max(N // nt, A - 1)
    for i in range(steps):
        if i < N // nt:
            columns(i)
        if i < A - 1:
            fresh.along_a(i + 1)
    for i in range(A):
        fresh.along_b(i)
    fresh.last()
    own_copy.wait()
    for copy in sends:
        copy.wait_send()


def body(A, B, T, cotangent, context, master, first_moment, second_moment):
    R, N = master.shape
    G = A * B
    dp = G * 2
    tk = cotangent.shape[0]
    cot = cotangent.T.reshape(G, 2, R, tk)
    ctx = context.reshape(T, tk, N)
    dma = pltpu.SemaphoreType.DMA
    hbm = pl.BlockSpec(memory_space=pl.ANY)
    vmem = pl.BlockSpec(memory_space=pltpu.VMEM)
    state = jax.ShapeDtypeStruct((R, N), F32)
    gathers = A - 1 + A * (B - 1) + A * B
    dctx, nmas, nmom, nvar, nw = pl.pallas_call(
        functools.partial(kernel, A, B, T, tk * T * dp),
        out_shape=(
            jax.ShapeDtypeStruct((T * tk, N), BF16),
            state, state, state,
            jax.ShapeDtypeStruct((dp, R, N), BF16),
        ),
        in_specs=[hbm, hbm, vmem, vmem, vmem],
        out_specs=(vmem, vmem, vmem, vmem, hbm),
        scratch_shapes=[
            pltpu.VMEM((T, tk, N), BF16),
            pltpu.VMEM((T, G, 2, R, tk), BF16),
            pltpu.VMEM((dp, R, N), BF16),
            pltpu.VMEM((2, R, N), F32),
            pltpu.VMEM((G, R, N), BF16),
            pltpu.VMEM((G, R, N), BF16),
            pltpu.VMEM((2, R, N), F32),
            pltpu.VMEM((A * (B - 1), R, N), BF16),
            pltpu.VMEM((A * (B - 1), R, N), BF16),
            pltpu.VMEM((A - 1, R, N), BF16),
            pltpu.VMEM((A - 1, R, N), BF16),
            pltpu.VMEM((R, N), BF16),
            dma((2,)),
            dma((G, T - 1)), dma((G, T - 1)),
            dma((gathers,)), dma((dp,)),
            dma((gathers,)), dma((dp,)),
            dma((G,)), dma((G,)),
            dma((A * (B - 1),)), dma((A * (B - 1),)),
            dma((A - 1,)), dma((A - 1,)),
        ],
        compiler_params=pltpu.CompilerParams(
            collective_id=0, has_side_effects=True, vmem_limit_bytes=60 * 1024 * 1024
        ),
    )(cot, ctx, master, first_moment, second_moment)
    return dctx, nmas, nmom, nvar, nw.reshape(dp * R, N)


def solution(mesh):
    dp, T = mesh.shape["dp"], mesh.shape["tensor"]
    A = 4
    B = dp // (2 * A)
    in_specs = (
        P(("dp", "tensor"), None),
        P("dp", "tensor"),
        P("dp", "tensor"),
        P("dp", "tensor"),
        P("dp", "tensor"),
    )
    out_specs = (
        P("dp", "tensor"),
        P("dp", "tensor"),
        P("dp", "tensor"),
        P("dp", "tensor"),
        P(None, "tensor"),
    )
    return jax.shard_map(
        functools.partial(body, A, B, T),
        mesh=mesh, in_specs=in_specs, out_specs=out_specs, check_vma=False,
    )
```

time: 486 us -> 215 us (0.44)
  the two profiles are of different devices: /device:TPU:0 before, /device:TPU:19 now
where the time goes in v1:
time: 215 us; the launch traced here: 214 us
  Pallas kernels  193 us (90%)
  local copies, waits for them, and re-layouts  20.9 us (10%)
    pallas_call x1, Pallas kernels, body(): pl.pallas_call(functools.partial(kernel, A, B, T, tk * T * dp), out_shape...  193 us
    unnamed x11, local copies, waits for them, and re-layouts  16.3 us
    transpose x1, local copies, waits for them, and re-layouts, body(): cot = cotangent.T.reshape(G, 2, R, tk)  4.65 us

profile of v1, /device:TPU:19, one launch (start us, length us, event | category | flops | bytes accessed | tf_op | source)
XLA Modules:
  0.0 214.3 jit_solution(15913388048198076828)
XLA Ops:
  0.6 4.6 %copy.10 = bf16[3072,512]{1,0:T(8,128)(2,1)} copy(bf16[3072,512]{0,1:T(8,128)(2,1)} %bitcast.6) | data formatting | bytes 6291456 | tf_op jit(solution)/shard_map/transpose | solution.py:250
  5.3 192.7 %shard_map.92 = (bf16[1024,1536]{1,0:T(8,128)(2,1)}, f32[192,1536]{1,0:T(8,128)}, f32[192,1536]{1,0:T(8,128)}, f32[192,1536]{1,0:T(8,128)}, bf16[16,192,1536]{2,1,0:T(8,128)(2,1)}) custom-call(bf16[8,2,192,512]{3,2,1,0:T(8,128)(2,1)} %bitcast.4, bf16[2,512,1536]{2,1,0:T(8,128)(2,1)} %bitcast.7, f32[192,1536]{1,0:T(8,128)} %mas.1, f32[192,1536]{1,0:T(8,128)} %mom.1, ...), custom_call_target="tpu_custom_call" | custom-call | tf_op jit(solution)/shard_map/pallas_call | solution.py:257
  198.0 0.0 copy-start.2
  198.0 3.9 %copy.16 = bf16[1024,1536]{1,0:T(8,128)(2,1)} copy(bf16[1024,1536]{1,0:T(8,128)(2,1)} %get-tuple-element.20) | data formatting | bytes 6291456
  201.9 0.0 copy-done.2
  201.9 0.0 copy-start.1
  201.9 1.0 copy.17
  202.9 0.7 copy-done.1
  203.6 0.0 copy-start
  203.6 1.0 copy.18
  204.6 0.7 copy-done
  205.3 1.0 copy.19
  206.3 8.0 %copy.20 = bf16[3072,1536]{1,0:T(8,128)(2,1)} copy(bf16[3072,1536]{1,0:T(8,128)(2,1)} %bitcast.5) | data formatting | bytes 18874368
Async XLA Ops:
  198.0 3.9 %copy-start.2 = (f32[192,1536]{1,0:T(8,128)S(1)}, f32[192,1536]{1,0:T(8,128)}, u32[]{:S(2)}) copy-start(f32[192,1536]{1,0:T(8,128)} %get-tuple-element.21) | copy-start | bytes 3538948
  201.9 1.7 copy-start.1
  203.6 1.7 copy-start

commit v2 on v1

--- a/solution.py
+++ b/solution.py
@@ -10,6 +10,7 @@
 STEP = 10
 F32 = jnp.float32
 BF16 = jnp.bfloat16
+PARTS = 8
 
 
 def tile_of(extent, most):
@@ -23,9 +24,9 @@
 def kernel(
     A, B, T, tokens,
     cot, ctx_in, mas, mom, var,
-    dctx, nmas, nmom, nvar, nw,
-    ctx, cotg, wfull, own, s1, r1, qown, s2, r2, s3, r3, nown,
-    loc_sem, cs_sem, cr_sem, ws_sem, wr_sem, ns_sem, nr_sem,
+    dctx, nmas, nmom, nvar, nw_out,
+    ctx, cotg, wfull, own, s1, r1, qown, s2, r2, s3, r3, nown, nw,
+    loc_sem, out_sem, cs_sem, cr_sem, ws_sem, wr_sem, ns_sem, nr_sem,
     s1_sem, r1_sem, s2_sem, r2_sem, s3_sem, r3_sem,
 ):
     G = A * B
@@ -48,11 +49,17 @@
     sib = flat(a, b, 1 - c)
     sends = []
 
-    def send(src, dst, ssem, rsem, where):
-        copy = pltpu.make_async_remote_copy(
+    held = []
+    H = 2 if R % 32 == 0 else 1
+
+    def remote(src, dst, ssem, rsem, where):
+        return pltpu.make_async_remote_copy(
             src_ref=src, dst_ref=dst, send_sem=ssem, recv_sem=rsem,
             device_id=where, device_id_type=pl.DeviceIdType.MESH,
         )
+
+    def send(*args):
+        copy = remote(*args)
         copy.start()
         sends.append(copy)
 
@@ -71,7 +78,8 @@
         pl.semaphore_signal(barrier, inc=1, device_id=where, device_id_type=pl.DeviceIdType.MESH)
     pl.semaphore_wait(barrier, len(peers))
 
-    order = [(ai, bi) for ai in [*range(1, A), 0] for bi in [*range(1, B), 0]]
+    far = sorted(range(1, A), key=lambda i: abs(2 * i - A))
+    order = [(ai, bi) for ai in [*far, 0] for bi in [*range(1, B), 0]]
 
     def group(k):
         ai, bi = order[k]
@@ -91,44 +99,87 @@
     cot_copy.start()
 
     class Gather:
-        def __init__(self, src, buf, ssem, rsem):
+        def __init__(self, src, buf, ssem, rsem, across_first):
             self.src, self.buf, self.ssem, self.rsem, self.n = src, buf, ssem, rsem, 0
-
-        def put(self, src, d, where):
-            send(src, self.buf.at[d], self.ssem.at[self.n], self.rsem.at[d], {"dp": where})
+            self.across_first = across_first
+
+        def rows(self, ref, h):
+            return ref.at[pl.ds(h * (R // H), R // H)]
+
+        def put(self, src, d, h, where, cond=None):
+            args = (
+                self.rows(src, h), self.rows(self.buf.at[d], h),
+                self.ssem.at[self.n], self.rsem.at[d * H + h], {"dp": where},
+            )
             self.n += 1
-
-        def first(self):
-            for i in range(1, A):
-                self.put(self.src, me, flat(a_of[i], b, c))
+            if cond is None:
+                send(*args)
+            else:
+                held.append((cond, args))
+
+                @pl.when(cond)
+                def _():
+                    remote(*args).start()
+
+        def line(self, src, d, h, up, cond=True):
+            if up:
+                self.put(src, d, h, flat(lax.rem(a + 1, A), b, c), jnp.logical_and(cond, a < A - 1))
+            else:
+                self.put(src, d, h, flat(lax.rem(a + A - 1, A), b, c), jnp.logical_and(cond, a > 0))
+
+        def first(self, h):
+            self.line(self.src, me, h, True)
+            self.line(self.src, me, h, False)
             for i in range(1, B):
-                self.put(self.src, me, flat(a, b_of[i], c))
-            self.put(self.src, me, sib)
-
-        def wait(self, d):
-            arrived(self.buf.at[d], self.ssem.at[0], self.rsem.at[d])
-
-        def along_a(self, i):
-            d = flat(a_of[A - i], b, c)
-            self.wait(d)
+                self.put(self.src, me, h, flat(a, b_of[i], c))
+            self.put(self.src, me, h, sib)
+
+        def wait(self, d, h):
+            arrived(self.rows(self.buf.at[d], h), self.ssem.at[0], self.rsem.at[d * H + h])
+
+        def across(self, h):
+            for j in range(1, B) if self.across_first[h] else ():
+                d = flat(a, b_of[j], c)
+                self.wait(d, h)
+                self.line(self.buf.at[d], d, h, True)
+                self.line(self.buf.at[d], d, h, False)
+                self.put(self.buf.at[d], d, h, sib)
+
+        def hop(self, s, h):
+            for j in range(B) if self.across_first[h] else (0,):
+                for up in (True, False):
+                    cond = a >= s if up else a + s < A
+                    d = flat(lax.rem(a + (A - s if up else s), A), b_of[j], c)
+
+                    @pl.when(cond)
+                    def _():
+                        self.wait(d, h)
+
+                    self.line(self.buf.at[d], d, h, up, cond)
+                    for i in range(1, B) if not self.across_first[h] else ():
+                        self.put(self.buf.at[d], d, h, flat(a, b_of[i], c), cond)
+                    self.put(self.buf.at[d], d, h, sib, cond)
+
+        def rest(self, h, s):
+            if self.across_first[h]:
+                return
             for j in range(1, B):
-                self.put(self.buf.at[d], d, flat(a, b_of[j], c))
-            self.put(self.buf.at[d], d, sib)
-
-        def along_b(self, i):
-            for j in range(1, B):
-                d = flat(a_of[(A - i) % A], b_of[j], c)
-                self.wait(d)
-                self.put(self.buf.at[d], d, sib)
-
-        def last(self):
+                d = flat(a_of[s], b_of[j], c)
+                self.wait(d, h)
+                self.put(self.buf.at[d], d, h, sib)
+
+        def last(self, then=lambda d: None):
             for i in range(A):
                 for j in range(B):
-                    self.wait(flat(a_of[i], b_of[j], 1 - c))
+                    d = flat(a_of[i], b_of[j], 1 - c)
+                    for h in range(H):
+                        self.wait(d, h)
+                    then(d)
 
     wfull[me] = mas[...].astype(BF16)
-    weights = Gather(wfull.at[me], wfull, ws_sem, wr_sem)
-    weights.first()
+    weights = Gather(wfull.at[me], wfull, ws_sem, wr_sem, [h == 1 for h in range(H)])
+    for h in range(H):
+        weights.first(h)
     ctx_copy.wait()
     cot_copy.wait()
 
@@ -184,33 +235,48 @@
         partial(g, c, to_own)
         if k:
             stage2(k - 1)
-        if k % B == B - 1 and k // B >= 1:
-            stage3(order[k - B][0])
-        if (k + 1) * (A - 1) // G > forwarded:
+        if k and k % B == 0:
+            stage3(order[k - 1][0])
+        if k == 1 or G == 1:
+            for h in range(H):
+                weights.across(h)
+        if k > 1 and (k - 1) * (A - 1) // (G - 2) > forwarded:
             forwarded += 1
-            weights.along_a(forwarded)
+            for h in range(H):
+                weights.hop(forwarded, h)
     stage2(G - 1)
     q = stage3(0)
     for i in range(1, A):
         arrived(r3.at[i - 1], s3_sem.at[i - 1], r3_sem.at[i - 1])
         q = q + r3[i - 1].astype(F32)
 
-    grad = q / jnp.float32(tokens)
-    new_first = 0.9 * mom[...] + 0.1 * grad
-    new_second = 0.95 * var[...] + 0.05 * grad * grad
-    update = new_first / (1.0 - 0.9**STEP) / (jnp.sqrt(new_second / (1.0 - 0.95**STEP)) + 1e-08)
-    new_master = mas[...] - 0.001 * update
-    nown[...] = new_master.astype(BF16)
-    fresh = Gather(nown, nw, ns_sem, nr_sem)
-    fresh.first()
-    nmom[...] = new_first
-    nvar[...] = new_second
-    nmas[...] = new_master
-    own_copy = pltpu.make_async_copy(nown, nw.at[me], loc_sem.at[0])
-    own_copy.start()
+    fresh = Gather(nown, nw, ns_sem, nr_sem, [False] * H)
+    for h in range(H):
+        rows = pl.ds(h * (R // H), R // H)
+        grad = q[h * (R // H) : (h + 1) * (R // H)] / jnp.float32(tokens)
+        new_first = 0.9 * mom[rows] + 0.1 * grad
+        new_second = 0.95 * var[rows] + 0.05 * grad * grad
+        update = new_first / (1.0 - 0.9**STEP) / (jnp.sqrt(new_second / (1.0 - 0.95**STEP)) + 1e-08)
+        new_master = mas[rows] - 0.001 * update
+        nown[rows] = new_master.astype(BF16)
+        fresh.first(h)
+        nmom[rows] = new_first
+        nvar[rows] = new_second
+        nmas[rows] = new_master
+    stores = []
+
+    def store(d, src=None):
+        src = nw.at[d] if src is None else src
+        stores.append(pltpu.make_async_copy(src, nw_out.at[d], out_sem.at[len(stores)]))
+        stores[-1].start()
+
+    store(me, nown)
 
     for i in range(A):
-        weights.along_b(i)
+        for h in range(H):
+            weights.rest(h, i)
+    for h in range(H):
+        fresh.hop(1, h)
     weights.last()
 
     mt = tile_of(tk, 256)
@@ -228,18 +294,50 @@
 
         lax.fori_loop(0, T * (tk // mt), tile, 0)
 
-    steps = max(N // nt, A - 1)
-    for i in range(steps):
+    for i in range(max(N // nt, A - 2)):
         if i < N // nt:
             columns(i)
-        if i < A - 1:
-            fresh.along_a(i + 1)
+        if i < A - 2:
+            for h in range(H):
+                fresh.hop(i + 2, h)
     for i in range(A):
-        fresh.along_b(i)
-    fresh.last()
-    own_copy.wait()
+        for h in range(H):
+            fresh.rest(h, i)
+    for i in range(A):
+        for j in range(B):
+            if i or j:
+                store(flat(a_of[i], b_of[j], c))
+    fresh.last(store)
+    for copy in stores:
+        copy.wait()
     for copy in sends:
         copy.wait_send()
+    for cond, args in held:
+
+        @pl.when(cond)
+        def _():
+            remote(*args).wait_send()
+
+
+def settle(*refs):
+    n = (len(refs) - 2) // 3
+    loads, stores = [], []
+    for i in range(n):
+        src, dst, held = refs[i], refs[n + i], refs[2 * n + i]
+        size = src.shape[0] // PARTS
+        parts = PARTS if size % 16 == 0 and size * PARTS == src.shape[0] and size > 64 else 1
+        size = src.shape[0] // parts
+        for j in range(parts):
+            rows = pl.ds(j * size, size)
+            loads.append(pltpu.make_async_copy(src.at[rows], held.at[rows], refs[-2].at[i, j]))
+            stores.append(pltpu.make_async_copy(held.at[rows], dst.at[rows], refs[-1].at[i, j]))
+    for load in loads:
+        load.start()
+    for load, store in zip(loads, stores):
+        load.wait()
+        store.start()
+    for store in stores:
+        store.wait()
 
 
 def body(A, B, T, cotangent, context, master, first_moment, second_moment):
@@ -253,7 +351,7 @@
     hbm = pl.BlockSpec(memory_space=pl.ANY)
     vmem = pl.BlockSpec(memory_space=pltpu.VMEM)
     state = jax.ShapeDtypeStruct((R, N), F32)
-    gathers = A - 1 + A * (B - 1) + A * B
+    gathers = 16 * A * B + 16
     dctx, nmas, nmom, nvar, nw = pl.pallas_call(
         functools.partial(kernel, A, B, T, tk * T * dp),
         out_shape=(
@@ -276,19 +374,29 @@
             pltpu.VMEM((A - 1, R, N), BF16),
             pltpu.VMEM((A - 1, R, N), BF16),
             pltpu.VMEM((R, N), BF16),
-            dma((2,)),
+            pltpu.VMEM((dp, R, N), BF16),
+            dma((2,)), dma((dp,)),
             dma((G, T - 1)), dma((G, T - 1)),
-            dma((gathers,)), dma((dp,)),
-            dma((gathers,)), dma((dp,)),
+            dma((gathers,)), dma((2 * dp,)),
+            dma((gathers,)), dma((2 * dp,)),
             dma((G,)), dma((G,)),
             dma((A * (B - 1),)), dma((A * (B - 1),)),
             dma((A - 1,)), dma((A - 1,)),
         ],
         compiler_params=pltpu.CompilerParams(
-            collective_id=0, has_side_effects=True, vmem_limit_bytes=60 * 1024 * 1024
+            collective_id=0, has_side_effects=True, vmem_limit_bytes=63 * 1024 * 1024
         ),
     )(cot, ctx, master, first_moment, second_moment)
-    return dctx, nmas, nmom, nvar, nw.reshape(dp * R, N)
+    results = (dctx, nmas, nmom, nvar, nw.reshape(dp * R, N))
+    return pl.pallas_call(
+        settle,
+        out_shape=tuple(jax.ShapeDtypeStruct(x.shape, x.dtype) for x in results),
+        in_specs=[hbm] * len(results),
+        out_specs=(hbm,) * len(results),
+        scratch_shapes=[pltpu.VMEM(x.shape, x.dtype) for x in results]
+        + [dma((len(results), PARTS)), dma((len(results), PARTS))],
+        compiler_params=pltpu.CompilerParams(vmem_limit_bytes=40 * 1024 * 1024),
+    )(*results)
 
 
 def solution(mesh):

time: 215 us -> 205 us (0.953)
  the two profiles are of different devices: /device:TPU:19 before, /device:TPU:0 now
where the time goes in v2:
time: 205 us
  Pallas kernels  194 us (95%)
  local copies, waits for them, and re-layouts  10.3 us (5%)
    pallas_call x1, Pallas kernels, body(): pl.pallas_call(functools.partial(kernel, A, B, T, tk * T * dp), out_shape...  181 us
    pallas_call x1, Pallas kernels, body(): pl.pallas_call(settle, out_shape=tuple((jax.ShapeDtypeStruct(x.shape, x.d...  12.5 us
    unnamed x8, local copies, waits for them, and re-layouts  5.69 us
    transpose x1, local copies, waits for them, and re-layouts, body(): cot = cotangent.T.reshape(G, 2, R, tk)  4.64 us

profile of v2, /device:TPU:0, one launch (start us, length us, event | category | flops | bytes accessed | tf_op | source)
XLA Modules:
  0.0 204.6 jit_solution(8894485013874708302)
XLA Ops:
  0.6 4.6 %copy.10 = bf16[3072,512]{1,0:T(8,128)(2,1)} copy(bf16[3072,512]{0,1:T(8,128)(2,1)} %bitcast.6) | data formatting | bytes 6291456 | tf_op jit(solution)/shard_map/transpose | solution.py:348
  5.3 181.1 %shard_map.92 = (bf16[1024,1536]{1,0:T(8,128)(2,1)}, f32[192,1536]{1,0:T(8,128)}, f32[192,1536]{1,0:T(8,128)}, f32[192,1536]{1,0:T(8,128)}, bf16[16,192,1536]{2,1,0:T(8,128)(2,1)}) custom-call(bf16[8,2,192,512]{3,2,1,0:T(8,128)(2,1)} %bitcast.4, bf16[2,512,1536]{2,1,0:T(8,128)(2,1)} %bitcast.7, f32[192,1536]{1,0:T(8,128)} %mas.1, f32[192,1536]{1,0:T(8,128)} %mom.1, ...), custom_call_target="tpu_custom_call" | custom-call | tf_op jit(solution)/shard_map/pallas_call | solution.py:355
  186.4 0.0 copy-start
  186.4 1.9 copy-done
  188.3 0.0 copy-start.1
  188.3 1.3 copy-done.1
  189.6 0.0 copy-start.2
  189.6 1.3 copy-done.2
  190.8 0.0 copy-start.3
  190.8 1.3 copy-done.3
  192.1 12.5 %shard_map.93 = (bf16[1024,1536]{1,0:T(8,128)(2,1)}, f32[192,1536]{1,0:T(8,128)}, f32[192,1536]{1,0:T(8,128)}, f32[192,1536]{1,0:T(8,128)}, bf16[3072,1536]{1,0:T(8,128)(2,1)}) custom-call(bf16[1024,1536]{1,0:T(8,128)(2,1)S(1)} %copy-done, f32[192,1536]{1,0:T(8,128)S(1)} %copy-done.1, f32[192,1536]{1,0:T(8,128)S(1)} %copy-done.2, f32[192,1536]{1,0:T(8,128)S(1)} %copy-done.3, ...), custom_call_target="tpu_custom_call" | custom-call | tf_op jit(solution)/shard_map/pallas_call | solution.py:391
Async XLA Ops:
  186.4 1.9 copy-start
  188.3 1.3 copy-start.1
  189.6 1.3 copy-start.2
  190.8 1.3 copy-start.3
